TPU v7x, 256 devices: a whole 4x4x8 slice. The times are simulated.
256 devices in a mesh: rx: 16 (over z, y_lo), ry: 4 (over x), ma: 4 (over y_hi, core).
Axes of the slice: x: 4, y: 4 (y_hi: 2, y_lo: 2; y = y_hi * 2 + y_lo), z: 8, core: 2. Of those that a mesh axis runs over, the one named last changes fastest.
Arguments:
- numerator: float32 [16, 4, 120, 13824], P('rx', 'ry', None, 'ma'), may hold values from -6 to 6
- weight: float32 [16, 4], P('rx', 'ry'), may hold values from 0.5 to 2
- inputs: bfloat16 [16, 4, 2, 256, 13824], P('rx', 'ry', None, None, 'ma'), may hold values from -0.125 to 0.125
- targets: float32 [16, 4, 2, 120, 256], P('rx', 'ry'), may hold values from -6 to 6
- first_moment: float32 [16, 4, 120, 13824], P('rx', 'ry', None, 'ma'), may hold values from -1.5 to 1.5
- second_moment: float32 [16, 4, 120, 13824], P('rx', 'ry', None, 'ma'), may hold values from 0.005 to 0.2
Outputs:
- new_numerator: float32 [16, 4, 120, 13824], P('rx', 'ry', None, 'ma')
- new_weight: float32 [16, 4], P('rx', 'ry')
- new_first: float32 [16, 4, 120, 13824], P('rx', 'ry', None, 'ma')
- new_second: float32 [16, 4, 120, 13824], P('rx', 'ry', None, 'ma')
All inputs are finite; a program needn't handle non-finite values.
Results may differ from a plain program's by a relative error of at most 0.0003.
Values sent between devices are 32-bit elements; how exact they have to be, the bound alone decides.
No kernel may reach another device: no remote copies, remote signals or barrier semaphores. Data moves between devices by JAX's collectives and lax.ppermute only.
A program may use at most 64 MiB of HBM per device.

v0:
```python
import jax
import jax.numpy as jnp
from jax import lax
from jax.sharding import PartitionSpec as P

PRIOR_STEPS = 100
BETA_ONE = 0.9
BETA_TWO = 0.999
LEARN_RATE = 0.05
EPSILON = 1e-08


def shifted(block, axis, distance):
    devices = range(lax.axis_size(axis))
    route = [((i - distance) % len(devices), i) for i in devices]
    return lax.ppermute(block, axis, route)


def adam_update(params, gradient, first, second, count):
    first = BETA_ONE * first + (1.0 - BETA_ONE) * gradient
    second = BETA_TWO * second + (1.0 - BETA_TWO) * gradient * gradient
    first_corr = 1.0 - BETA_ONE**count
    second_corr = 1.0 - BETA_TWO**count
    params = params - LEARN_RATE * (first / first_corr) / (jnp.sqrt(second / second_corr) + EPSILON)
    return (params, first, second)


def mix_row(values, scales):
    left_values, left_scales = shifted((values, scales), "rx", 1)
    right_values, right_scales = shifted((values, scales), "rx", -1)
    return (
        (values + left_values + right_values) / 3.0,
        (scales + left_scales + right_scales) / 3.0,
    )


def mix_column(values, scales):
    left_values, left_scales = shifted((values, scales), "ry", 1)
    right_values, right_scales = shifted((values, scales), "ry", -1)
    return (
        (values + left_values + right_values) / 3.0,
        (scales + left_scales + right_scales) / 3.0,
    )


def one_round(values, scales, first, second, inputs_narrow, targets_round, mixer, count):
    inputs_round = inputs_narrow.astype(jnp.float32)
    values, scales = mixer(values, scales)
    params = values[0, 0] / scales[0, 0]
    partial_pred = jnp.einsum("cf,tf->ct", params, inputs_round, precision=lax.Precision.HIGHEST)
    predicted = lax.psum(partial_pred, "ma")
    gradient = jnp.einsum(
        "ct,tf->cf", predicted - targets_round, inputs_round, precision=lax.Precision.HIGHEST
    )
    params, new_first, new_second = adam_update(params, gradient, first[0, 0], second[0, 0], count)
    values = (scales[0, 0] * params)[None, None]
    return (values, scales, new_first[None, None], new_second[None, None])


def local(numerator, weight, inputs, targets, first_moment, second_moment):
    values, scales, first, second = one_round(
        numerator,
        weight,
        first_moment,
        second_moment,
        inputs[0, 0, 0],
        targets[0, 0, 0],
        mix_row,
        PRIOR_STEPS + 1,
    )
    values, scales, first, second = one_round(
        values,
        scales,
        first,
        second,
        inputs[0, 0, 1],
        targets[0, 0, 1],
        mix_column,
        PRIOR_STEPS + 2,
    )
    return (values, scales, first, second)


def solution(mesh):
    return jax.shard_map(
        local,
        mesh=mesh,
        in_specs=(
            P("rx", "ry", None, "ma"),
            P("rx", "ry"),
            P("rx", "ry", None, None, "ma"),
            P("rx", "ry", None, None, None),
            P("rx", "ry", None, "ma"),
            P("rx", "ry", None, "ma"),
        ),
        out_specs=(
            P("rx", "ry", None, "ma"),
            P("rx", "ry"),
            P("rx", "ry", None, "ma"),
            P("rx", "ry", None, "ma"),
        ),
        check_vma=False,
    )
```

profile of v0, /device:TPU:1, one launch (start us, length us, event | category | flops | bytes accessed | tf_op | source)
XLA Modules:
  0.0 253.2 jit_solution(13335298537395719774)
XLA Ops:
  7.2 0.0 all-reduce.3.cloned.1.call-start
  7.2 2.2 collective-permute-start.4
  9.4 5.4 %collective-permute-start.5 = (f32[1,1,120,3456]{3,2,1,0:T(8,128)}, f32[1,1,120,3456]{3,2,1,0:T(8,128)S(1)}, u32[]{:S(2)}, u32[]{:S(2)}) collective-permute-start(f32[1,1,120,3456]{3,2,1,0:T(8,128)} %param.6), channel_id=1, source_target_pairs={{16,0},{32,16},{48,32},{64,48},{80,64},{96,80},{112,96},{128,112},... | collective-permute-start | bytes 4976648 | tf_op jit(solution)/shard_map/ppermute | solution.py:16
  14.8 0.0 collective-permute-start
  14.8 3.6 %collective-permute-start.1 = (f32[1,1]{1,0:T(1,128)}, f32[1,1]{1,0:T(1,128)}, u32[]{:S(2)}, u32[]{:S(2)}) collective-permute-start(f32[1,1]{1,0:T(1,128)} %param.7), channel_id=1, source_target_pairs={{16,0},{32,16},{48,32},{64,48},{80,64},{96,80},{112,96},{128,112},... | collective-permute-start | bytes 20 | tf_op jit(solution)/shard_map/ppermute | solution.py:16
  19.1 60.9 %collective-permute-done = f32[1,1]{1,0:T(1,128)} collective-permute-done((f32[1,1]{1,0:T(1,128)}, f32[1,1]{1,0:T(1,128)}, u32[]{:S(2)}, u32[]{:S(2)}) %collective-permute-start) | collective-permute-done | bytes 36 | tf_op jit(solution)/shard_map/ppermute | solution.py:16
  80.6 1.3 collective-permute-done.1
  82.6 0.0 collective-permute-done.4
  82.6 0.0 copy-start.3
  82.6 0.0 collective-permute-done.5
  82.6 0.0 copy-start.4
  82.6 1.1 copy-done.3
  83.8 0.5 copy-done.4
  84.3 4.4 %fusion.6 = f32[120,256]{1,0:T(8,128)} fusion(bf16[1,1,2,256,3456]{4,3,2,1,0:T(8,128)(2,1)} %param.8, f32[1,1,120,3456]{3,2,1,0:T(8,128)S(1)} %collective-permute-done.5, f32[1,1,120,3456]{3,2,1,0:T(8,128)} %param.6, f32[1,1,120,3456]{3,2,1,0:T(8,128)S(1)} %collective-permute-done.4, f32[]{:T(128)} %bitcast.1), kind=kOutput, calls=%fused_computation.8 | convolution fusion | flops 1275678720 | bytes 6869504 | tf_op jit(solution)/shard_map/cf,tf->ct/dot_general | solution.py:50
  88.7 0.0 all-reduce.3.cloned.1.call-update
  88.8 0.0 copy-start
  88.8 0.0 all-reduce.5.cloned.1.call-start
  88.8 49.7 %all-reduce.3.cloned.1.call-done = f32[120,256]{1,0:T(8,128)} async-done(((f32[120,256]{1,0:T(8,128)}), f32[120,256]{1,0:T(8,128)}) %all-reduce.3.cloned.1.call-update) | async-done | bytes 122896 | tf_op jit(solution)/shard_map/psum | solution.py:51
  138.6 2.5 fusion.4
  141.1 0.0 copy-done
  141.1 0.0 copy-start.5
  141.1 4.5 %fusion.15 = f32[1,1,120,3456]{3,2,1,0:T(8,128)S(1)} fusion(f32[]{:T(128)} %bitcast.1, f32[120,3456]{1,0:T(8,128)S(1)} %fusion.4, f32[1,1,120,3456]{3,2,1,0:T(8,128)} %param.10, f32[1,1,120,3456]{3,2,1,0:T(8,128)} %param.11, f32[1,1,120,3456]{3,2,1,0:T(8,128)} %copy-done.4, f32[1,1,120,3456]{3,2,1,0:T(8,128)S(1)} %copy-done, f32[1,1,120,3456]{3,2,1,0:T(8,128)} %copy-done.3), kind=kLoop, calls=%fused_computation.20 | loop fusion | flops 7050240 | bytes 11612164 | tf_op jit(solution)/shard_map/broadcast_in_dim | solution.py:56
  145.6 0.0 copy-start.2
  145.6 2.5 collective-permute-start.7
  148.1 0.0 collective-permute-start.6
  148.1 35.5 %collective-permute-start.3 = (f32[1,1]{1,0:T(1,128)}, f32[1,1]{1,0:T(1,128)}, u32[]{:S(2)}, u32[]{:S(2)}) collective-permute-start(f32[1,1]{1,0:T(1,128)} %div.50), channel_id=1, source_target_pairs={{4,0},{8,4},{12,8},{0,12},{5,1},{9,5},{13,9},{1,13},{6,2},{10,6},{... | collective-permute-start | bytes 20 | tf_op jit(solution)/shard_map/ppermute | solution.py:16
  183.6 0.7 collective-permute-start.2
  184.3 3.2 %collective-permute-done.2 = f32[1,1]{1,0:T(1,128)} collective-permute-done((f32[1,1]{1,0:T(1,128)}, f32[1,1]{1,0:T(1,128)}, u32[]{:S(2)}, u32[]{:S(2)}) %collective-permute-start.2) | collective-permute-done | bytes 36 | tf_op jit(solution)/shard_map/ppermute | solution.py:16
  188.2 0.0 collective-permute-done.3
  188.8 0.0 collective-permute-done.7
  188.8 0.0 copy-start.6
  188.8 0.0 collective-permute-done.6
  188.8 0.0 copy-start.7
  188.8 0.0 copy-done.2
  188.8 1.1 copy-done.6
  190.0 0.5 copy-done.7
  190.5 0.0 copy-done.5
  190.5 0.0 copy-start.1
  190.5 2.4 fusion.2
  192.9 0.0 all-reduce.5.cloned.1.call-update
  193.0 43.8 %all-reduce.5.cloned.1.call-done = f32[120,256]{1,0:T(8,128)} async-done(((f32[120,256]{1,0:T(8,128)}), f32[120,256]{1,0:T(8,128)}) %all-reduce.5.cloned.1.call-update) | async-done | bytes 122896 | tf_op jit(solution)/shard_map/psum | solution.py:51
  236.8 0.0 copy-done.1
  236.8 8.4 %fusion.21 = (f32[1,1,120,3456]{3,2,1,0:T(8,128)}, f32[1,1,120,3456]{3,2,1,0:T(8,128)}, f32[1,1,120,3456]{3,2,1,0:T(8,128)}) fusion(f32[120,3456]{1,0:T(8,128)S(1)} %fusion.4, f32[1,1,120,3456]{3,2,1,0:T(8,128)S(1)} %copy-done.1, f32[1,1,120,3456]{3,2,1,0:T(8,128)} %param.10, f32[]{:T(128)} %bitcast, f32[1,1,120,3456]{3,2,1,0:T(8,128)} %copy-done.6, ...), kind=kOutput, calls=%fused_computation.29 | convolution fusion | flops 1284003840 | bytes 16946176 | tf_op jit(solution)/shard_map/ct,tf->cf/dot_general | solution.py:52
Async XLA Ops:
  7.2 131.4 %all-reduce.3.cloned.1.call-start = ((), (), s32[]{:S(2)}) async-start(), calls=%async_computation | async-start | bytes 245760 | tf_op jit(solution)/shard_map/psum | solution.py:51
  7.2 75.4 %collective-permute-start.4 = (f32[1,1,120,3456]{3,2,1,0:T(8,128)}, f32[1,1,120,3456]{3,2,1,0:T(8,128)S(1)}, u32[]{:S(2)}, u32[]{:S(2)}) collective-permute-start(f32[1,1,120,3456]{3,2,1,0:T(8,128)} %param.6), channel_id=1, source_target_pairs={{240,0},{0,16},{16,32},{32,48},{48,64},{64,80},{80,96},{96,112},{1... | collective-permute-start | bytes 4976648 | tf_op jit(solution)/shard_map/ppermute | solution.py:16
  9.4 73.2 %collective-permute-start.5 = (f32[1,1,120,3456]{3,2,1,0:T(8,128)}, f32[1,1,120,3456]{3,2,1,0:T(8,128)S(1)}, u32[]{:S(2)}, u32[]{:S(2)}) collective-permute-start(f32[1,1,120,3456]{3,2,1,0:T(8,128)} %param.6), channel_id=1, source_target_pairs={{16,0},{32,16},{48,32},{64,48},{80,64},{96,80},{112,96},{128,112},... | collective-permute-start | bytes 4976648 | tf_op jit(solution)/shard_map/ppermute | solution.py:16
  14.8 65.2 %collective-permute-start = (f32[1,1]{1,0:T(1,128)}, f32[1,1]{1,0:T(1,128)}, u32[]{:S(2)}, u32[]{:S(2)}) collective-permute-start(f32[1,1]{1,0:T(1,128)} %param.7), channel_id=1, source_target_pairs={{240,0},{0,16},{16,32},{32,48},{48,64},{64,80},{80,96},{96,112},{1... | collective-permute-start | bytes 20 | tf_op jit(solution)/shard_map/ppermute | solution.py:16
  14.8 67.1 %collective-permute-start.1 = (f32[1,1]{1,0:T(1,128)}, f32[1,1]{1,0:T(1,128)}, u32[]{:S(2)}, u32[]{:S(2)}) collective-permute-start(f32[1,1]{1,0:T(1,128)} %param.7), channel_id=1, source_target_pairs={{16,0},{32,16},{48,32},{64,48},{80,64},{96,80},{112,96},{128,112},... | collective-permute-start | bytes 20 | tf_op jit(solution)/shard_map/ppermute | solution.py:16
  82.6 1.2 copy-start.3
  82.6 1.7 copy-start.4
  88.8 52.3 %copy-start = (f32[1,1,120,3456]{3,2,1,0:T(8,128)S(1)}, f32[1,1,120,3456]{3,2,1,0:T(8,128)}, u32[]{:S(2)}) copy-start(f32[1,1,120,3456]{3,2,1,0:T(8,128)} %param.6) | copy-start | bytes 4976644
  88.8 148.0 %all-reduce.5.cloned.1.call-start = ((), (), s32[]{:S(2)}) async-start(), calls=%async_computation.1 | async-start | bytes 245760 | tf_op jit(solution)/shard_map/psum | solution.py:51
  141.1 49.4 %copy-start.5 = (bf16[1,1,2,256,3456]{4,3,2,1,0:T(8,128)(2,1)S(1)}, bf16[1,1,2,256,3456]{4,3,2,1,0:T(8,128)(2,1)}, u32[]{:S(2)}) copy-start(bf16[1,1,2,256,3456]{4,3,2,1,0:T(8,128)(2,1)} %param.8) | copy-start | bytes 10616836
  145.6 43.2 %copy-start.2 = (f32[1,1,120,3456]{3,2,1,0:T(8,128)}, f32[1,1,120,3456]{3,2,1,0:T(8,128)S(1)}, u32[]{:S(2)}) copy-start(f32[1,1,120,3456]{3,2,1,0:T(8,128)S(1)} %fusion.15) | copy-start | bytes 4976644
  145.6 43.2 %collective-permute-start.7 = (f32[1,1,120,3456]{3,2,1,0:T(8,128)S(1)}, f32[1,1,120,3456]{3,2,1,0:T(8,128)S(1)}, u32[]{:S(2)}, u32[]{:S(2)}) collective-permute-start(f32[1,1,120,3456]{3,2,1,0:T(8,128)S(1)} %fusion.15), channel_id=1, source_target_pairs={{4,0},{8,4},{12,8},{0,12},{5,1},{9,5},{13,9},{1,13},{6,2},{10,6},{... | collective-permute-start | bytes 4976648 | tf_op jit(solution)/shard_map/ppermute | solution.py:16
  148.1 40.7 %collective-permute-start.6 = (f32[1,1,120,3456]{3,2,1,0:T(8,128)S(1)}, f32[1,1,120,3456]{3,2,1,0:T(8,128)S(1)}, u32[]{:S(2)}, u32[]{:S(2)}) collective-permute-start(f32[1,1,120,3456]{3,2,1,0:T(8,128)S(1)} %fusion.15), channel_id=1, source_target_pairs={{12,0},{0,4},{4,8},{8,12},{13,1},{1,5},{5,9},{9,13},{14,2},{2,6},{... | collective-permute-start | bytes 4976648 | tf_op jit(solution)/shard_map/ppermute | solution.py:16
  148.1 40.1 %collective-permute-start.3 = (f32[1,1]{1,0:T(1,128)}, f32[1,1]{1,0:T(1,128)}, u32[]{:S(2)}, u32[]{:S(2)}) collective-permute-start(f32[1,1]{1,0:T(1,128)} %div.50), channel_id=1, source_target_pairs={{4,0},{8,4},{12,8},{0,12},{5,1},{9,5},{13,9},{1,13},{6,2},{10,6},{... | collective-permute-start | bytes 20 | tf_op jit(solution)/shard_map/ppermute | solution.py:16
  183.6 3.9 %collective-permute-start.2 = (f32[1,1]{1,0:T(1,128)}, f32[1,1]{1,0:T(1,128)}, u32[]{:S(2)}, u32[]{:S(2)}) collective-permute-start(f32[1,1]{1,0:T(1,128)} %div.50), channel_id=1, source_target_pairs={{12,0},{0,4},{4,8},{8,12},{13,1},{1,5},{5,9},{9,13},{14,2},{2,6},{... | collective-permute-start | bytes 20 | tf_op jit(solution)/shard_map/ppermute | solution.py:16
  188.8 1.2 copy-start.6
  188.8 1.7 copy-start.7
  190.5 46.3 %copy-start.1 = (f32[1,1,120,3456]{3,2,1,0:T(8,128)S(1)}, f32[1,1,120,3456]{3,2,1,0:T(8,128)}, u32[]{:S(2)}) copy-start(f32[1,1,120,3456]{3,2,1,0:T(8,128)} %param.11) | copy-start | bytes 4976644
Sparse Core Ops, SparseCore 0:
  88.9 49.6 all-reduce.2
  193.1 43.6 all-reduce.4
where the time goes:
time: 253 us
  waiting for transfers between devices  159 us (63%)
  starting transfers between devices  50 us (20%)
  between operations  18.5 us (7%)
  matrix products  17.7 us (7%)
  other arithmetic  4.47 us (2%)
  local copies, waits for them, and re-layouts  3.39 us (1%)
    psum x2, waiting for transfers between devices, one_round(): predicted = lax.psum(partial_pred, 'ma')  93.6 us
    ppermute x8, waiting for transfers between devices, shifted(): return lax.ppermute(block, axis, route)  65.5 us
    ppermute x8, starting transfers between devices, shifted(): return lax.ppermute(block, axis, route)  49.9 us
    dot_general x2, matrix products, one_round(): jnp.einsum('ct,tf->cf', predicted - targets_round, inputs_round, precisio...  10.9 us
    dot_general x2, matrix products, one_round(): jnp.einsum('cf,tf->ct', params, inputs_round, precision=lax.Precision.HIG...  6.85 us
  transfers between devices with their start and end apart: 10, of which 5 were waited for; matrix products, arithmetic and copies ran while one was open for 0% of the time, Pallas kernels for 0%

commit v1 on v0

--- a/solution.py
+++ b/solution.py
@@ -48,7 +48,7 @@
     values, scales = mixer(values, scales)
     params = values[0, 0] / scales[0, 0]
     partial_pred = jnp.einsum("cf,tf->ct", params, inputs_round, precision=lax.Precision.HIGHEST)
-    predicted = lax.psum(partial_pred, "ma")
+    predicted = jnp.sum(lax.all_gather(partial_pred, "ma"), axis=0)
     gradient = jnp.einsum(
         "ct,tf->cf", predicted - targets_round, inputs_round, precision=lax.Precision.HIGHEST
     )

time: 253 us -> 163 us (0.64)
  waiting for transfers between devices: 159 us -> 65.5 us
  blocking collectives: 0 us -> 20.3 us
  between operations: 18.5 us -> 5.08 us
  local copies, waits for them, and re-layouts: 3.39 us -> 0.06 us
    psum x2 -> x0, waiting for transfers between devices: 93.6 us -> none  [one_round(): predicted = lax.psum(partial_pred, 'ma')]
    all_gather x0 -> x2, blocking collectives: none -> 20.3 us  [one_round(): predicted = jnp.sum(lax.all_gather(partial_pred, 'ma'), axis=0)]
    unnamed x16 -> x20, local copies, waits for them, and re-layouts: 3.39 us -> 0.06 us
  transfers between devices with their start and end apart: 10 -> 8, of which waited for: 5 -> 3; matrix products, arithmetic and copies ran while one was open for 0% -> 0% of each run, Pallas kernels for 0% -> 0%
where the time goes in v1:
time: 163 us
  waiting for transfers between devices  65.5 us (40%)
  starting transfers between devices  50 us (31%)
  blocking collectives  20.3 us (12%)
  matrix products  18.1 us (11%)
  between operations  5.08 us (3%)
  other arithmetic  3.57 us (2%)
    ppermute x8, waiting for transfers between devices, shifted(): return lax.ppermute(block, axis, route)  65.5 us
    ppermute x8, starting transfers between devices, shifted(): return lax.ppermute(block, axis, route)  50 us
    all_gather x2, blocking collectives, one_round(): predicted = jnp.sum(lax.all_gather(partial_pred, 'ma'), axis=0)  20.3 us
    dot_general x2, matrix products, one_round(): jnp.einsum('ct,tf->cf', predicted - targets_round, inputs_round, precisio...  11.3 us
    dot_general x2, matrix products, one_round(): jnp.einsum('cf,tf->ct', params, inputs_round, precision=lax.Precision.HIG...  6.78 us
    broadcast_in_dim x1, other arithmetic, one_round(): values = (scales[0, 0] * params)[None, None]  3.51 us
  transfers between devices with their start and end apart: 8, of which 3 were waited for; matrix products, arithmetic and copies ran while one was open for 0% of the time, Pallas kernels for 0%

profile of v1, /device:TPU:1, one launch (start us, length us, event | category | flops | bytes accessed | tf_op | source)
XLA Modules:
  0.0 162.5 jit_solution(1620925597276284029)
XLA Ops:
  0.6 2.2 %collective-permute-start.4 = (f32[1,1,120,3456]{3,2,1,0:T(8,128)}, f32[1,1,120,3456]{3,2,1,0:T(8,128)S(1)}, u32[]{:S(2)}, u32[]{:S(2)}) collective-permute-start(f32[1,1,120,3456]{3,2,1,0:T(8,128)} %param.6), channel_id=1, source_target_pairs={{240,0},{0,16},{16,32},{32,48},{48,64},{64,80},{80,96},{96,112},{1... | collective-permute-start | bytes 4976648 | tf_op jit(solution)/shard_map/ppermute | solution.py:16
  2.8 5.4 %collective-permute-start.5 = (f32[1,1,120,3456]{3,2,1,0:T(8,128)}, f32[1,1,120,3456]{3,2,1,0:T(8,128)S(1)}, u32[]{:S(2)}, u32[]{:S(2)}) collective-permute-start(f32[1,1,120,3456]{3,2,1,0:T(8,128)} %param.6), channel_id=1, source_target_pairs={{16,0},{32,16},{48,32},{64,48},{80,64},{96,80},{112,96},{128,112},... | collective-permute-start | bytes 4976648 | tf_op jit(solution)/shard_map/ppermute | solution.py:16
  8.2 0.0 collective-permute-start
  8.2 3.6 %collective-permute-start.1 = (f32[1,1]{1,0:T(1,128)}, f32[1,1]{1,0:T(1,128)}, u32[]{:S(2)}, u32[]{:S(2)}) collective-permute-start(f32[1,1]{1,0:T(1,128)} %param.7), channel_id=1, source_target_pairs={{16,0},{32,16},{48,32},{64,48},{80,64},{96,80},{112,96},{128,112},... | collective-permute-start | bytes 20 | tf_op jit(solution)/shard_map/ppermute | solution.py:16
  12.5 60.9 %collective-permute-done = f32[1,1]{1,0:T(1,128)} collective-permute-done((f32[1,1]{1,0:T(1,128)}, f32[1,1]{1,0:T(1,128)}, u32[]{:S(2)}, u32[]{:S(2)}) %collective-permute-start) | collective-permute-done | bytes 36 | tf_op jit(solution)/shard_map/ppermute | solution.py:16
  74.0 1.3 collective-permute-done.1
  76.0 0.0 collective-permute-done.4
  76.0 0.0 copy-start.4
  76.0 0.0 collective-permute-done.5
  76.0 0.0 copy-start.5
  76.0 0.0 copy-start.2
  76.0 5.0 %fusion.6 = f32[120,256]{1,0:T(8,128)S(1)} fusion(bf16[1,1,2,256,3456]{4,3,2,1,0:T(8,128)(2,1)} %param.8, f32[1,1,120,3456]{3,2,1,0:T(8,128)S(1)} %collective-permute-done.5, f32[1,1,120,3456]{3,2,1,0:T(8,128)} %param.6, f32[1,1,120,3456]{3,2,1,0:T(8,128)S(1)} %collective-permute-done.4, f32[]{:T(128)} %bitcast.1), kind=kOutput, calls=%fused_computation.8 | convolution fusion | flops 1275678720 | bytes 6869504 | tf_op jit(solution)/shard_map/cf,tf->ct/dot_general | solution.py:50
  81.0 0.0 copy-done.4
  81.0 0.0 copy-done.5
  81.0 10.6 %all-gather = f32[480,256]{1,0:T(8,128)S(1)} all-gather(f32[120,256]{1,0:T(8,128)S(1)} %fusion.6), channel_id=2, replica_groups=mesh['rx'=16,'ry'=4,'ma'=4] {'ma'}, dimensions={0}, use_global_device_ids=true | all-gather | bytes 614400 | tf_op jit(solution)/shard_map/all_gather | solution.py:51
  91.6 0.0 copy-start
  91.7 0.0 copy-start.1
  91.7 2.6 %fusion.4 = f32[120,3456]{1,0:T(8,128)S(1)} fusion(bf16[1,1,2,256,3456]{4,3,2,1,0:T(8,128)(2,1)} %param.8, f32[120,256]{1,0:T(8,128)S(1)} %reduce_sum.22, f32[1,1,2,120,256]{4,3,2,1,0:T(8,128)} %param.9), kind=kOutput, calls=%fused_computation.6 | convolution fusion | flops 1274050560 | bytes 3674112 | tf_op jit(solution)/shard_map/ct,tf->cf/dot_general | solution.py:52
  94.2 0.0 copy-done.2
  94.3 0.0 copy-done
  94.3 0.0 copy-done.1
  94.3 0.0 copy-start.6
  94.3 3.5 %fusion.15 = f32[1,1,120,3456]{3,2,1,0:T(8,128)S(1)} fusion(f32[]{:T(128)} %bitcast.1, f32[120,3456]{1,0:T(8,128)S(1)} %fusion.4, f32[1,1,120,3456]{3,2,1,0:T(8,128)S(1)} %copy-done.2, f32[1,1,120,3456]{3,2,1,0:T(8,128)S(1)} %copy-done.1, f32[1,1,120,3456]{3,2,1,0:T(8,128)} %copy-done.5, f32[1,1,120,3456]{3,2,1,0:T(8,128)S(1)} %copy-done, ...), kind=kLoop, calls=%fused_computation.20 | loop fusion | flops 7050240 | bytes 11612164 | tf_op jit(solution)/shard_map/broadcast_in_dim | solution.py:56
  97.8 0.0 copy-start.3
  97.8 2.6 %collective-permute-start.7 = (f32[1,1,120,3456]{3,2,1,0:T(8,128)S(1)}, f32[1,1,120,3456]{3,2,1,0:T(8,128)S(1)}, u32[]{:S(2)}, u32[]{:S(2)}) collective-permute-start(f32[1,1,120,3456]{3,2,1,0:T(8,128)S(1)} %fusion.15), channel_id=1, source_target_pairs={{4,0},{8,4},{12,8},{0,12},{5,1},{9,5},{13,9},{1,13},{6,2},{10,6},{... | collective-permute-start | bytes 4976648 | tf_op jit(solution)/shard_map/ppermute | solution.py:16
  100.4 0.0 collective-permute-start.6
  100.4 35.5 %collective-permute-start.3 = (f32[1,1]{1,0:T(1,128)}, f32[1,1]{1,0:T(1,128)}, u32[]{:S(2)}, u32[]{:S(2)}) collective-permute-start(f32[1,1]{1,0:T(1,128)} %div.50), channel_id=1, source_target_pairs={{4,0},{8,4},{12,8},{0,12},{5,1},{9,5},{13,9},{1,13},{6,2},{10,6},{... | collective-permute-start | bytes 20 | tf_op jit(solution)/shard_map/ppermute | solution.py:16
  135.9 0.7 collective-permute-start.2
  136.6 3.2 %collective-permute-done.2 = f32[1,1]{1,0:T(1,128)} collective-permute-done((f32[1,1]{1,0:T(1,128)}, f32[1,1]{1,0:T(1,128)}, u32[]{:S(2)}, u32[]{:S(2)}) %collective-permute-start.2) | collective-permute-done | bytes 36 | tf_op jit(solution)/shard_map/ppermute | solution.py:16
  140.4 0.0 collective-permute-done.3
  141.0 0.0 collective-permute-done.7
  141.0 0.0 copy-start.8
  141.0 0.0 collective-permute-done.6
  141.1 0.0 copy-start.9
  141.1 0.0 copy-done.6
  141.1 0.0 copy-start.7
  141.1 1.8 %fusion.2 = f32[120,256]{1,0:T(8,128)S(1)} fusion(bf16[1,1,2,256,3456]{4,3,2,1,0:T(8,128)(2,1)S(1)} %copy-done.6, f32[1,1,120,3456]{3,2,1,0:T(8,128)S(1)} %collective-permute-done.7, f32[1,1,120,3456]{3,2,1,0:T(8,128)S(1)} %fusion.15, f32[1,1,120,3456]{3,2,1,0:T(8,128)S(1)} %collective-permute-done.6, f32[]{:T(128)} %bitcast), kind=kOutput, calls=%fused_computation.4 | convolution fusion | flops 1275678720 | bytes 6868996 | tf_op jit(solution)/shard_map/cf,tf->ct/dot_general | solution.py:50
  142.9 0.0 copy-done.3
  142.9 0.0 copy-done.8
  142.9 0.0 copy-done.9
  142.9 9.7 %all-gather.1 = f32[480,256]{1,0:T(8,128)S(1)} all-gather(f32[120,256]{1,0:T(8,128)S(1)} %fusion.2), channel_id=3, replica_groups=mesh['rx'=16,'ry'=4,'ma'=4] {'ma'}, dimensions={0}, use_global_device_ids=true | all-gather | bytes 614400 | tf_op jit(solution)/shard_map/all_gather | solution.py:51
  152.7 0.0 copy-done.7
  152.7 8.7 %fusion.21 = (f32[1,1,120,3456]{3,2,1,0:T(8,128)}, f32[1,1,120,3456]{3,2,1,0:T(8,128)}, f32[1,1,120,3456]{3,2,1,0:T(8,128)}) fusion(f32[120,3456]{1,0:T(8,128)S(1)} %fusion.4, f32[1,1,120,3456]{3,2,1,0:T(8,128)} %param.11, f32[1,1,120,3456]{3,2,1,0:T(8,128)} %param.10, f32[]{:T(128)} %bitcast, f32[1,1,120,3456]{3,2,1,0:T(8,128)} %copy-done.8, ...), kind=kOutput, calls=%fused_computation.29 | convolution fusion | flops 1284003840 | bytes 16946176 | tf_op jit(solution)/shard_map/ct,tf->cf/dot_general | solution.py:52
  (2 shorter events, 0.1 us)
Async XLA Ops:
  0.6 75.3 %collective-permute-start.4 = (f32[1,1,120,3456]{3,2,1,0:T(8,128)}, f32[1,1,120,3456]{3,2,1,0:T(8,128)S(1)}, u32[]{:S(2)}, u32[]{:S(2)}) collective-permute-start(f32[1,1,120,3456]{3,2,1,0:T(8,128)} %param.6), channel_id=1, source_target_pairs={{240,0},{0,16},{16,32},{32,48},{48,64},{64,80},{80,96},{96,112},{1... | collective-permute-start | bytes 4976648 | tf_op jit(solution)/shard_map/ppermute | solution.py:16
  2.8 73.1 %collective-permute-start.5 = (f32[1,1,120,3456]{3,2,1,0:T(8,128)}, f32[1,1,120,3456]{3,2,1,0:T(8,128)S(1)}, u32[]{:S(2)}, u32[]{:S(2)}) collective-permute-start(f32[1,1,120,3456]{3,2,1,0:T(8,128)} %param.6), channel_id=1, source_target_pairs={{16,0},{32,16},{48,32},{64,48},{80,64},{96,80},{112,96},{128,112},... | collective-permute-start | bytes 4976648 | tf_op jit(solution)/shard_map/ppermute | solution.py:16
  8.2 65.2 %collective-permute-start = (f32[1,1]{1,0:T(1,128)}, f32[1,1]{1,0:T(1,128)}, u32[]{:S(2)}, u32[]{:S(2)}) collective-permute-start(f32[1,1]{1,0:T(1,128)} %param.7), channel_id=1, source_target_pairs={{240,0},{0,16},{16,32},{32,48},{48,64},{64,80},{80,96},{96,112},{1... | collective-permute-start | bytes 20 | tf_op jit(solution)/shard_map/ppermute | solution.py:16
  8.2 67.1 %collective-permute-start.1 = (f32[1,1]{1,0:T(1,128)}, f32[1,1]{1,0:T(1,128)}, u32[]{:S(2)}, u32[]{:S(2)}) collective-permute-start(f32[1,1]{1,0:T(1,128)} %param.7), channel_id=1, source_target_pairs={{16,0},{32,16},{48,32},{64,48},{80,64},{96,80},{112,96},{128,112},... | collective-permute-start | bytes 20 | tf_op jit(solution)/shard_map/ppermute | solution.py:16
  76.0 5.0 %copy-start.4 = (f32[1,1,120,3456]{3,2,1,0:T(8,128)}, f32[1,1,120,3456]{3,2,1,0:T(8,128)S(1)}, u32[]{:S(2)}) copy-start(f32[1,1,120,3456]{3,2,1,0:T(8,128)S(1)} %collective-permute-done.4) | copy-start | bytes 4976644
  76.0 5.0 %copy-start.5 = (f32[1,1,120,3456]{3,2,1,0:T(8,128)}, f32[1,1,120,3456]{3,2,1,0:T(8,128)S(1)}, u32[]{:S(2)}) copy-start(f32[1,1,120,3456]{3,2,1,0:T(8,128)S(1)} %collective-permute-done.5) | copy-start | bytes 4976644
  76.0 18.3 %copy-start.2 = (f32[1,1,120,3456]{3,2,1,0:T(8,128)S(1)}, f32[1,1,120,3456]{3,2,1,0:T(8,128)}, u32[]{:S(2)}) copy-start(f32[1,1,120,3456]{3,2,1,0:T(8,128)} %param.10) | copy-start | bytes 4976644
  91.6 2.6 %copy-start = (f32[1,1,120,3456]{3,2,1,0:T(8,128)S(1)}, f32[1,1,120,3456]{3,2,1,0:T(8,128)}, u32[]{:S(2)}) copy-start(f32[1,1,120,3456]{3,2,1,0:T(8,128)} %param.6) | copy-start | bytes 4976644
  91.7 2.6 %copy-start.1 = (f32[1,1,120,3456]{3,2,1,0:T(8,128)S(1)}, f32[1,1,120,3456]{3,2,1,0:T(8,128)}, u32[]{:S(2)}) copy-start(f32[1,1,120,3456]{3,2,1,0:T(8,128)} %param.11) | copy-start | bytes 4976644
  94.3 46.8 %copy-start.6 = (bf16[1,1,2,256,3456]{4,3,2,1,0:T(8,128)(2,1)S(1)}, bf16[1,1,2,256,3456]{4,3,2,1,0:T(8,128)(2,1)}, u32[]{:S(2)}) copy-start(bf16[1,1,2,256,3456]{4,3,2,1,0:T(8,128)(2,1)} %param.8) | copy-start | bytes 10616836
  97.8 45.1 %copy-start.3 = (f32[1,1,120,3456]{3,2,1,0:T(8,128)}, f32[1,1,120,3456]{3,2,1,0:T(8,128)S(1)}, u32[]{:S(2)}) copy-start(f32[1,1,120,3456]{3,2,1,0:T(8,128)S(1)} %fusion.15) | copy-start | bytes 4976644
  97.8 43.2 %collective-permute-start.7 = (f32[1,1,120,3456]{3,2,1,0:T(8,128)S(1)}, f32[1,1,120,3456]{3,2,1,0:T(8,128)S(1)}, u32[]{:S(2)}, u32[]{:S(2)}) collective-permute-start(f32[1,1,120,3456]{3,2,1,0:T(8,128)S(1)} %fusion.15), channel_id=1, source_target_pairs={{4,0},{8,4},{12,8},{0,12},{5,1},{9,5},{13,9},{1,13},{6,2},{10,6},{... | collective-permute-start | bytes 4976648 | tf_op jit(solution)/shard_map/ppermute | solution.py:16
  100.4 40.7 %collective-permute-start.6 = (f32[1,1,120,3456]{3,2,1,0:T(8,128)S(1)}, f32[1,1,120,3456]{3,2,1,0:T(8,128)S(1)}, u32[]{:S(2)}, u32[]{:S(2)}) collective-permute-start(f32[1,1,120,3456]{3,2,1,0:T(8,128)S(1)} %fusion.15), channel_id=1, source_target_pairs={{12,0},{0,4},{4,8},{8,12},{13,1},{1,5},{5,9},{9,13},{14,2},{2,6},{... | collective-permute-start | bytes 4976648 | tf_op jit(solution)/shard_map/ppermute | solution.py:16
  100.4 40.1 %collective-permute-start.3 = (f32[1,1]{1,0:T(1,128)}, f32[1,1]{1,0:T(1,128)}, u32[]{:S(2)}, u32[]{:S(2)}) collective-permute-start(f32[1,1]{1,0:T(1,128)} %div.50), channel_id=1, source_target_pairs={{4,0},{8,4},{12,8},{0,12},{5,1},{9,5},{13,9},{1,13},{6,2},{10,6},{... | collective-permute-start | bytes 20 | tf_op jit(solution)/shard_map/ppermute | solution.py:16
  135.9 3.9 %collective-permute-start.2 = (f32[1,1]{1,0:T(1,128)}, f32[1,1]{1,0:T(1,128)}, u32[]{:S(2)}, u32[]{:S(2)}) collective-permute-start(f32[1,1]{1,0:T(1,128)} %div.50), channel_id=1, source_target_pairs={{12,0},{0,4},{4,8},{8,12},{13,1},{1,5},{5,9},{9,13},{14,2},{2,6},{... | collective-permute-start | bytes 20 | tf_op jit(solution)/shard_map/ppermute | solution.py:16
  141.0 1.9 %copy-start.8 = (f32[1,1,120,3456]{3,2,1,0:T(8,128)}, f32[1,1,120,3456]{3,2,1,0:T(8,128)S(1)}, u32[]{:S(2)}) copy-start(f32[1,1,120,3456]{3,2,1,0:T(8,128)S(1)} %collective-permute-done.7) | copy-start | bytes 4976644
  141.1 1.9 %copy-start.9 = (f32[1,1,120,3456]{3,2,1,0:T(8,128)}, f32[1,1,120,3456]{3,2,1,0:T(8,128)S(1)}, u32[]{:S(2)}) copy-start(f32[1,1,120,3456]{3,2,1,0:T(8,128)S(1)} %collective-permute-done.6) | copy-start | bytes 4976644
  141.1 11.6 %copy-start.7 = (f32[1,1,2,120,256]{4,3,2,1,0:T(8,128)S(1)}, f32[1,1,2,120,256]{4,3,2,1,0:T(8,128)}, u32[]{:S(2)}) copy-start(f32[1,1,2,120,256]{4,3,2,1,0:T(8,128)} %param.9) | copy-start | bytes 737284
